TPU v7x, 32 devices: a whole 2x2x4 slice. The times are simulated.
32 devices in a mesh: seq: 8 (over z, x), head: 4 (over y, core).
Axes of the slice: x: 2, y: 2, z: 4, core: 2. Of those that a mesh axis runs over, the one named last changes fastest.
Arguments:
- queries: bfloat16 [1024, 4096], P('seq', 'head'), may hold values from -150 to 150
- neighbours: bfloat16 [8, 128, 8, 448], P(None, 'seq', None, 'head'), may hold values from -6 to 6
- key_weight: bfloat16 [448, 4096], P(None, 'head'), may hold values from -0.25 to 0.25
- value_weight: bfloat16 [448, 4096], P(None, 'head'), may hold values from -0.25 to 0.25
- counts: int32 [16], P('seq'), may hold values from 1 to 4, as said below
- slot_map: int32 [8, 8], P('seq'), may hold values from 0 to 7, each once within a row
- d_attended: bfloat16 [1024, 4096], P('seq', 'head'), may hold values from -6 to 6
Outputs:
- attended: bfloat16 [1024, 4096], P('seq', 'head')
- d_queries: bfloat16 [1024, 4096], P('seq', 'head')
- d_neighbours: bfloat16 [8, 128, 8, 448], P(None, 'seq', None, 'head')
Inputs may be any that keep to these rules, and one draw needn't show every extreme that they name: `counts`: every span has at least one neighbour; some span has 4. `slot_map`: each row is a permutation; entry c * 4 + j names the slot that holds neighbour j of local span c, and only entries with j below the span's count are used.
All inputs are finite; a program needn't handle non-finite values.
Results may differ from a plain program's by a relative error of at most 0.03.
Values may be sent and summed in bfloat16 or wider, within the bound.
A program may use at most 64 MiB of HBM per device.

v0:
```python
import jax
import jax.numpy as jnp
from jax import lax
from jax.sharding import PartitionSpec as P

HDIM = 128
SPAN = 64
NB_LEN = 128
MAX_NB = 4
CH_DEV = 2
SLOTS = 8


def present_table(count_row, slot_row):
    chosen = slot_row.reshape(CH_DEV, MAX_NB)
    ranks = jnp.arange(MAX_NB, dtype=jnp.int32)
    valid = ranks[None, :] < count_row[:, None]
    slot_ids = jnp.arange(SLOTS, dtype=jnp.int32)
    hits = valid[:, :, None] & (chosen[:, :, None] == slot_ids[None, None, :])
    return jnp.any(hits, axis=1)


def per_device(queries, neighbours, key_weight, value_weight, counts, slot_map, d_attended):
    total_rows = NB_LEN * SLOTS
    enc_local = neighbours.shape[3]
    width_local = key_weight.shape[1]
    heads_local = width_local // HDIM
    token_count = queries.shape[0]
    highest = lax.Precision.HIGHEST
    arrived = lax.all_to_all(neighbours, "seq", split_axis=0, concat_axis=1, tiled=True)
    flat_rows = arrived.reshape(total_rows, enc_local)
    portion = lax.all_gather(flat_rows, "head", axis=1, tiled=True)
    key_sum = jnp.dot(portion, key_weight, preferred_element_type=jnp.float32)
    value_sum = jnp.dot(portion, value_weight, preferred_element_type=jnp.float32)
    keys = key_sum.reshape(total_rows, heads_local, HDIM)
    values = value_sum.astype(jnp.bfloat16).reshape(total_rows, heads_local, HDIM)
    present = present_table(counts, slot_map[0])
    allowed = jnp.tile(jnp.repeat(present, SPAN, axis=0), (1, NB_LEN))
    factor = 1.0 / HDIM**0.5
    query_heads = queries.reshape(token_count, heads_local, HDIM)
    grad_heads = d_attended.reshape(token_count, heads_local, HDIM)
    scores = (
        jnp.einsum(
            "thd,rhd->htr",
            query_heads.astype(jnp.float32),
            keys,
            precision=highest,
            preferred_element_type=jnp.float32,
        )
        * factor
    )
    scores = jnp.where(allowed[None, :, :], scores, -jnp.inf)
    top = jnp.max(scores, axis=-1, keepdims=True)
    expo = jnp.exp(scores - top)
    probs = expo / jnp.sum(expo, axis=-1, keepdims=True)
    probs_b = probs.astype(jnp.bfloat16)
    attended = jnp.einsum("htr,rhd->thd", probs_b, values, preferred_element_type=jnp.float32)
    attended = attended.astype(jnp.bfloat16).reshape(token_count, width_local)
    dprobs = jnp.einsum("thd,rhd->htr", grad_heads, values, preferred_element_type=jnp.float32)
    inner = jnp.sum(probs * dprobs, axis=-1, keepdims=True)
    dscores = (probs * (dprobs - inner)).astype(jnp.bfloat16)
    d_queries = (
        jnp.einsum(
            "htr,rhd->thd",
            dscores.astype(jnp.float32),
            keys,
            precision=highest,
            preferred_element_type=jnp.float32,
        )
        * factor
    )
    d_queries = d_queries.astype(jnp.bfloat16).reshape(token_count, width_local)
    d_keys = (
        jnp.einsum("htr,thd->rhd", dscores, query_heads, preferred_element_type=jnp.float32)
        * factor
    )
    d_keys = d_keys.astype(jnp.bfloat16).reshape(total_rows, width_local)
    d_values = jnp.einsum("htr,thd->rhd", probs_b, grad_heads, preferred_element_type=jnp.float32)
    d_values = d_values.astype(jnp.bfloat16).reshape(total_rows, width_local)
    contract = (((1,), (1,)), ((), ()))
    partial_value = lax.dot_general(
        d_keys, key_weight, contract, preferred_element_type=jnp.float32
    )
    partial_value = partial_value + lax.dot_general(
        d_values, value_weight, contract, preferred_element_type=jnp.float32
    )
    summed = lax.psum(partial_value.astype(jnp.bfloat16), "head").astype(jnp.float32)
    own_part = lax.dynamic_slice_in_dim(summed, lax.axis_index("head") * enc_local, enc_local, 1)
    grad_rows = own_part.astype(jnp.bfloat16).reshape(1, NB_LEN, SLOTS, enc_local)
    d_neighbours = lax.all_to_all(grad_rows, "seq", split_axis=1, concat_axis=0, tiled=True)
    return (attended, d_queries, d_neighbours)


def solution(mesh):
    in_specs = (
        P("seq", "head"),
        P(None, "seq", None, "head"),
        P(None, "head"),
        P(None, "head"),
        P("seq"),
        P("seq", None),
        P("seq", "head"),
    )
    out_specs = (P("seq", "head"), P("seq", "head"), P(None, "seq", None, "head"))
    return jax.shard_map(
        per_device, mesh=mesh, in_specs=in_specs, out_specs=out_specs, check_vma=False
    )
```

profile of v0, /device:TPU:0, one launch (start us, length us, event | category | flops | bytes accessed | tf_op | source)
XLA Modules:
  0.0 117.4 jit_solution(8158770567810797703)
XLA Ops:
  7.2 0.0 copy-start
  7.2 7.4 %all-to-all-start = ((bf16[8,16,8,112]{3,2,1,0:T(8,128)(2,1)}), bf16[8,16,8,112]{3,2,1,0:T(8,128)(2,1)S(1)}, u32[]{:S(2)}, u32[]{:S(2)}) async-start(bf16[8,16,8,112]{3,2,1,0:T(8,128)(2,1)} %param.8), calls=%async_computation | async-start | bytes 524288 | tf_op jit(solution)/shard_map/all_to_all | solution.py:30
  14.6 0.0 all-reduce.2.cloned.1.call-start
  14.6 0.7 iota_compare_fusion.1
  15.4 1.1 copy.98
  16.5 0.5 broadcast.30
  17.0 1.3 %reduce.3 = s32[8]{0:T(128)S(1)} reduce(s32[1,8]{1,0:T(1,128)} %param.12, s32[]{:T(128)} %broadcast.30), dimensions={0}, to_apply=%param.12.reduce_sub_computation.3 | reduce | bytes 68 | tf_op args[5]
  18.3 0.1 eq.15
  18.4 0.1 fusion.13
  18.5 0.1 copy.74
  18.6 0.1 broadcast_in_dim.14
  18.7 0.1 tile.9
  18.8 1.1 copy.99
  19.9 3.6 %all-to-all-done = bf16[8,16,8,112]{3,2,1,0:T(8,128)(2,1)S(1)} async-done(((bf16[8,16,8,112]{3,2,1,0:T(8,128)(2,1)}), bf16[8,16,8,112]{3,2,1,0:T(8,128)(2,1)S(1)}, u32[]{:S(2)}, u32[]{:S(2)}) %all-to-all-start) | async-done | bytes 229408 | tf_op jit(solution)/shard_map/all_to_all | solution.py:30
  23.5 0.1 copy.73
  23.6 9.3 %all_gather.3 = bf16[1024,448]{0,1:T(8,128)(2,1)S(1)} all-gather(bf16[1024,112]{0,1:T(8,128)(2,1)S(1)} %copy.73), channel_id=1, replica_groups=mesh['seq'=8,'head'=4] {'head'}, dimensions={1}, use_global_device_ids=true | all-gather | bytes 1146880 | tf_op jit(solution)/shard_map/all_gather | solution.py:32
  33.0 2.5 %convolution_convert_fusion = bf16[1024,1024]{0,1:T(8,128)(2,1)S(1)} fusion(bf16[1024,448]{0,1:T(8,128)(2,1)S(1)} %all_gather.3, bf16[448,1024]{1,0:T(8,128)(2,1)} %param.10), kind=kOutput, calls=%fused_computation.14 | convolution fusion | flops 940572672 | bytes 3932160 | tf_op jit(solution)/shard_map/dot_general | solution.py:34
  35.5 0.0 copy-done
  35.5 0.0 copy-start.4
  35.5 1.3 %fusion.17 = f32[1024,1024]{0,1:T(8,128)S(1)} fusion(bf16[1024,448]{0,1:T(8,128)(2,1)S(1)} %all_gather.3, bf16[448,1024]{1,0:T(8,128)(2,1)S(1)} %copy-done), kind=kOutput, calls=%fused_computation.32 | convolution fusion | flops 939524096 | bytes 6029312 | tf_op jit(solution)/shard_map/dot_general | solution.py:33
  36.8 0.0 copy-start.1
  36.8 1.9 %copy-done.1 = f32[1024,1024]{0,1:T(8,128)} copy-done((f32[1024,1024]{0,1:T(8,128)}, f32[1024,1024]{0,1:T(8,128)S(1)}, u32[]{:S(2)}) %copy-start.1) | copy-done | bytes 4194328
  38.7 3.5 %fusion.18 = f32[8,1024,128]{2,1,0:T(8,128)S(1)} fusion(f32[1024,8,128]{0,2,1:T(8,128)S(1)} %bitcast.63, bf16[128,8,128]{0,2,1:T(8,128)(2,1)S(1)} %bitcast.65), kind=kOutput, calls=%fused_computation.33 | convolution fusion | flops 1610612736 | bytes 8650752 | tf_op jit(solution)/shard_map/thd,rhd->htr/dot_general | solution.py:43
  42.2 1.9 %fusion.16 = (f32[8,128]{1,0:T(8,128)S(1)}, f32[8,128,1024]{1,2,0:T(8,128)S(1)}) fusion(f32[8,1024,128]{2,1,0:T(8,128)S(1)} %fusion.18, pred[128,1024]{0,1:T(8,128)(4,1)S(1)} %broadcast_bitcast_fusion), kind=kOutput, calls=%fused_computation.31 | output fusion | flops 6292479 | bytes 8523776 | tf_op jit(solution)/shard_map/sub | solution.py:54
  44.2 0.0 copy-start.2
  44.2 2.5 %convolution_convert_fusion.1 = bf16[8,1024,128]{1,2,0:T(8,128)(2,1)} fusion(bf16[128,8,128]{0,2,1:T(8,128)(2,1)S(1)} %bitcast.71, f32[8,128,1024]{1,2,0:T(8,128)S(1)} %get-tuple-element.19, f32[8,128]{1,0:T(8,128)S(1)} %get-tuple-element.18), kind=kOutput, calls=%fused_computation.15 | convolution fusion | flops 271581184 | bytes 6557696 | tf_op jit(solution)/shard_map/htr,thd->rhd/dot_general | solution.py:78
  46.7 0.0 copy-done.4
  46.7 1.1 fusion.1
  47.7 0.0 copy-done.2
  47.7 0.6 fusion.3
  48.3 2.1 %fusion.8 = bf16[1024,8,128]{2,0,1:T(8,128)(2,1)} fusion(bf16[8,128,1024]{1,2,0:T(8,128)(2,1)S(1)} %fusion.3, bf16[128,8,128]{0,2,1:T(8,128)(2,1)S(1)} %bitcast.66), kind=kOutput, calls=%fused_computation.17 | convolution fusion | flops 270532608 | bytes 4456448 | tf_op jit(solution)/shard_map/htr,thd->rhd/dot_general | solution.py:74
  50.4 3.9 %copy.84 = bf16[1024,8,128]{0,2,1:T(8,128)(2,1)} copy(bf16[1024,8,128]{2,0,1:T(8,128)(2,1)} %fusion.8) | data formatting | bytes 4194304 | tf_op jit(solution)/shard_map/convert_element_type | solution.py:77
  54.3 0.0 copy-start.3
  54.3 2.9 %fusion.19 = f32[1024,448]{0,1:T(8,128)S(1)} fusion(bf16[448,1024]{1,0:T(8,128)(2,1)S(1)} %copy-done, bf16[1024,1024]{0,1:T(8,128)(2,1)} %bitcast.67), kind=kOutput, calls=%fused_computation.34 | convolution fusion | flops 939524096 | bytes 4849664 | tf_op jit(solution)/shard_map/dot_general | solution.py:81
  57.2 0.0 copy-done.3
  57.2 0.0 copy-done.5
  57.2 2.0 %add_convert_fusion = bf16[1024,448]{0,1:T(8,128)(2,1)} fusion(f32[1024,448]{0,1:T(8,128)S(1)} %fusion.19, bf16[448,1024]{1,0:T(8,128)(2,1)S(1)} %copy-done.3, bf16[1024,1024]{0,1:T(8,128)(2,1)S(1)} %bitcast.76), kind=kOutput, calls=%fused_computation.16 | convolution fusion | flops 940441600 | bytes 5767168 | tf_op jit(solution)/shard_map/dot_general | solution.py:84
  59.2 0.0 all-reduce.2.cloned.1.call-update
  59.3 33.8 %all-reduce.2.cloned.1.call-done = bf16[1024,448]{0,1:T(8,128)(2,1)} async-done(((bf16[1024,448]{0,1:T(8,128)(2,1)}), bf16[1024,448]{0,1:T(8,128)(2,1)}) %all-reduce.2.cloned.1.call-update) | async-done | bytes 917520 | tf_op jit(solution)/shard_map/psum | solution.py:87
  93.0 1.0 convert_convert_fusion
  94.0 0.8 copy.87
  94.8 5.5 %all-to-all-start.1 = ((bf16[1,128,8,112]{3,2,0,1:T(8,128)(2,1)}), bf16[1,128,8,112]{3,2,0,1:T(8,128)(2,1)S(1)}, u32[]{:S(2)}, u32[]{:S(2)}) async-start(bf16[1,128,8,112]{3,2,0,1:T(8,128)(2,1)} %bitcast.15), calls=%async_computation.1 | async-start | bytes 524288 | tf_op jit(solution)/shard_map/all_to_all | solution.py:90
  100.3 3.5 %convolution_convert_fusion.2 = bf16[8,128,128]{2,1,0:T(8,128)(2,1)S(1)} fusion(bf16[1024,8,128]{0,2,1:T(8,128)(2,1)} %bitcast.75, f32[8,128,1024]{1,2,0:T(8,128)} %copy-done.2, f32[8,128]{1,0:T(8,128)S(1)} %get-tuple-element.18), kind=kOutput, calls=%fused_computation.19 | convolution fusion | flops 270663680 | bytes 6557696 | tf_op jit(solution)/shard_map/htr,rhd->thd/dot_general | solution.py:57
  103.9 0.9 copy.89
  104.7 4.3 %fusion.9 = bf16[8,128,128]{2,1,0:T(8,128)(2,1)S(1)} fusion(f32[1024,8,128]{0,2,1:T(8,128)} %bitcast.64, bf16[8,128,1024]{1,2,0:T(8,128)(2,1)S(1)} %fusion.3), kind=kOutput, calls=%fused_computation.20 | convolution fusion | flops 1610874880 | bytes 6553600 | tf_op jit(solution)/shard_map/htr,rhd->thd/dot_general | solution.py:63
  109.0 0.9 copy.90
  109.9 0.0 all-to-all-done.1
  109.9 0.7 copy.102
  (2 shorter events, 0.0 us)
Async XLA Ops:
  7.2 28.3 %copy-start = (bf16[448,1024]{1,0:T(8,128)(2,1)S(1)}, bf16[448,1024]{1,0:T(8,128)(2,1)}, u32[]{:S(2)}) copy-start(bf16[448,1024]{1,0:T(8,128)(2,1)} %param.9) | copy-start | bytes 2752516
  7.2 16.3 %all-to-all-start = ((bf16[8,16,8,112]{3,2,1,0:T(8,128)(2,1)}), bf16[8,16,8,112]{3,2,1,0:T(8,128)(2,1)S(1)}, u32[]{:S(2)}, u32[]{:S(2)}) async-start(bf16[8,16,8,112]{3,2,1,0:T(8,128)(2,1)} %param.8), calls=%async_computation | async-start | bytes 524288 | tf_op jit(solution)/shard_map/all_to_all | solution.py:30
  14.6 78.4 %all-reduce.2.cloned.1.call-start = ((), (), s32[]{:S(2)}) async-start(), calls=%async_computation.2 | async-start | bytes 1835008 | tf_op jit(solution)/shard_map/psum | solution.py:87
  35.5 11.2 %copy-start.4 = (bf16[1024,1024]{0,1:T(8,128)(2,1)}, bf16[1024,1024]{0,1:T(8,128)(2,1)S(1)}, u32[]{:S(2)}) copy-start(bf16[1024,1024]{0,1:T(8,128)(2,1)S(1)} %convolution_convert_fusion) | copy-start | bytes 6291460
  36.8 1.9 %copy-start.1 = (f32[1024,1024]{0,1:T(8,128)}, f32[1024,1024]{0,1:T(8,128)S(1)}, u32[]{:S(2)}) copy-start(f32[1024,1024]{0,1:T(8,128)S(1)} %fusion.17) | copy-start | bytes 12582916
  44.2 3.5 %copy-start.2 = (f32[8,128,1024]{1,2,0:T(8,128)}, f32[8,128,1024]{1,2,0:T(8,128)S(1)}, u32[]{:S(2)}) copy-start(f32[8,128,1024]{1,2,0:T(8,128)S(1)} %get-tuple-element.19) | copy-start | bytes 12582916
  54.3 2.9 %copy-start.3 = (bf16[448,1024]{1,0:T(8,128)(2,1)S(1)}, bf16[448,1024]{1,0:T(8,128)(2,1)}, u32[]{:S(2)}) copy-start(bf16[448,1024]{1,0:T(8,128)(2,1)} %param.10) | copy-start | bytes 2752516
  54.3 2.9 %copy-start.5 = (bf16[8,1024,128]{1,2,0:T(8,128)(2,1)S(1)}, bf16[8,1024,128]{1,2,0:T(8,128)(2,1)}, u32[]{:S(2)}) copy-start(bf16[8,1024,128]{1,2,0:T(8,128)(2,1)} %convolution_convert_fusion.1) | copy-start | bytes 6291460
  94.8 15.1 %all-to-all-start.1 = ((bf16[1,128,8,112]{3,2,0,1:T(8,128)(2,1)}), bf16[1,128,8,112]{3,2,0,1:T(8,128)(2,1)S(1)}, u32[]{:S(2)}, u32[]{:S(2)}) async-start(bf16[1,128,8,112]{3,2,0,1:T(8,128)(2,1)} %bitcast.15), calls=%async_computation.1 | async-start | bytes 524288 | tf_op jit(solution)/shard_map/all_to_all | solution.py:90
Sparse Core Ops, SparseCore 0:
  59.4 33.5 all-reduce.1
where the time goes:
time: 118 us; the launch traced here: 117 us
  waiting for transfers between devices  37.3 us (32%)
  matrix products  25.6 us (22%)
  between operations  14.2 us (12%)
  starting transfers between devices  12.9 us (11%)
  local copies, waits for them, and re-layouts  12.4 us (11%)
  blocking collectives  9.34 us (8%)
  other arithmetic  5.63 us (5%)
    psum x1, waiting for transfers between devices, per_device(): lax.psum(partial_value.astype(jnp.bfloat16), 'head').astype(jnp.float32)  33.8 us
    all_gather x1, blocking collectives, per_device(): portion = lax.all_gather(flat_rows, 'head', axis=1, tiled=True)  9.34 us
    all_to_all x1, starting transfers between devices, per_device(): lax.all_to_all(neighbours, 'seq', split_axis=0, concat_axis=1, tiled=True)  7.4 us
    all_to_all x1, starting transfers between devices, per_device(): lax.all_to_all(grad_rows, 'seq', split_axis=1, concat_axis=0, tiled=True)  5.51 us
    unnamed x16, local copies, waits for them, and re-layouts  4.86 us
    dot_general x1, matrix products, per_device(): jnp.einsum('htr,rhd->thd', dscores.astype(jnp.float32), keys, precision=h...  4.31 us
    convert_element_type x1, local copies, waits for them, and re-layouts, per_device(): d_keys = d_keys.astype(jnp.bfloat16).reshape(total_rows, width_local)  3.91 us
    all_to_all x1, waiting for transfers between devices, per_device(): lax.all_to_all(neighbours, 'seq', split_axis=0, concat_axis=1, tiled=True)  3.57 us
  transfers between devices with their start and end apart: 3, of which 2 were waited for; matrix products, arithmetic and copies ran while one was open for 13% of the time, Pallas kernels for 0%

commit v1 on v0

--- a/solution.py
+++ b/solution.py
@@ -1,6 +1,11 @@
+import functools
+import math
+
 import jax
 import jax.numpy as jnp
 from jax import lax
+from jax.experimental import pallas as pl
+from jax.experimental.pallas import tpu as pltpu
 from jax.sharding import PartitionSpec as P
 
 HDIM = 128
@@ -9,6 +14,10 @@
 MAX_NB = 4
 CH_DEV = 2
 SLOTS = 8
+LANES = 128
+CORES = 2
+MESH_ID = pl.DeviceIdType.MESH
+VMEM = pltpu.VMEM
 
 
 def present_table(count_row, slot_row):
@@ -20,7 +29,7 @@
     return jnp.any(hits, axis=1)
 
 
-def per_device(queries, neighbours, key_weight, value_weight, counts, slot_map, d_attended):
+def per_device_plain(queries, neighbours, key_weight, value_weight, counts, slot_map, d_attended):
     total_rows = NB_LEN * SLOTS
     enc_local = neighbours.shape[3]
     width_local = key_weight.shape[1]
@@ -91,7 +100,348 @@
     return (attended, d_queries, d_neighbours)
 
 
+def positions(n_seq):
+    me = lax.axis_index("seq")
+    head = lax.axis_index("head")
+    y = head // CORES
+    core = head % CORES
+    across = (1 - y) * CORES + core
+    beside = y * CORES + (1 - core)
+    return me, head, y, core, across, beside
+
+
+def greet(n_seq, me, head, across, beside):
+    barrier = pltpu.get_barrier_semaphore()
+    for k in range(1, n_seq):
+        pl.semaphore_signal(
+            barrier, inc=1, device_id=((me + k) % n_seq, head), device_id_type=MESH_ID
+        )
+    for peer in (across, beside):
+        pl.semaphore_signal(barrier, inc=1, device_id=(me, peer), device_id_type=MESH_ID)
+    pl.semaphore_wait(barrier, n_seq + 1)
+
+
+def gather_kernel(n_seq, block, nb_ref, rows_ref, packed, own_sem, s_send, s_recv, y_send, y_recv, c_send, c_recv, f_send, f_recv):
+    me, head, y, core, across, beside = positions(n_seq)
+    enc_local = nb_ref.shape[1]
+    packed[...] = jnp.zeros_like(packed)
+    packed[:, :enc_local] = nb_ref[...]
+    greet(n_seq, me, head, across, beside)
+
+    def rows_of(quarter, owner):
+        return rows_ref.at[quarter, pl.ds(pl.multiple_of(owner * block, block), block), :]
+
+    def remote(src, dst, send, recv, device):
+        return pltpu.make_async_remote_copy(
+            src_ref=src,
+            dst_ref=dst,
+            send_sem=send,
+            recv_sem=recv,
+            device_id=device,
+            device_id_type=MESH_ID,
+        )
+
+    own = pltpu.make_async_copy(
+        packed.at[pl.ds(pl.multiple_of(me * block, block), block), :], rows_of(head, me), own_sem
+    )
+    own.start()
+    sent = []
+    for k in range(n_seq - 1, 0, -1):
+        to = (me + k) % n_seq
+        copy = remote(
+            packed.at[pl.ds(pl.multiple_of(to * block, block), block), :],
+            rows_of(head, me),
+            s_send.at[k],
+            s_recv.at[k],
+            (to, head),
+        )
+        copy.start()
+        sent.append((k, copy))
+    pending = []
+    order = [0] + [k for k, _ in sent]
+    arrivals = dict(sent)
+    own.wait()
+    for k in order:
+        owner = (me + n_seq - k) % n_seq
+        if k > 0:
+            arrivals[k].wait_recv()
+        over = remote(rows_of(head, owner), rows_of(head, owner), y_send.at[k], y_recv.at[k], (me, across))
+        over.start()
+        side = remote(rows_of(head, owner), rows_of(head, owner), c_send.at[k], c_recv.at[k], (me, beside))
+        side.start()
+        pending.append((owner, k, over, side))
+    forwards = []
+    for owner, k, over, side in pending:
+        over.wait_recv()
+        forward = remote(
+            rows_of(across, owner), rows_of(across, owner), f_send.at[k], f_recv.at[k], (me, beside)
+        )
+        forward.start()
+        forwards.append(forward)
+    for owner, k, over, side in pending:
+        side.wait_recv()
+    for forward in forwards:
+        forward.wait_recv()
+    for k, copy in sent:
+        copy.wait_send()
+    for owner, k, over, side in pending:
+        over.wait_send()
+        side.wait_send()
+    for forward in forwards:
+        forward.wait_send()
+
+
+def gather(n_seq, block, rows):
+    dma = pltpu.SemaphoreType.DMA
+    return pl.pallas_call(
+        functools.partial(gather_kernel, n_seq, block),
+        out_shape=jax.ShapeDtypeStruct((4, n_seq * block, LANES), jnp.bfloat16),
+        in_specs=[pl.BlockSpec(memory_space=VMEM)],
+        out_specs=pl.BlockSpec(memory_space=VMEM),
+        scratch_shapes=[pltpu.VMEM((n_seq * block, LANES), jnp.bfloat16), dma]
+        + [dma((n_seq,)) for _ in range(8)],
+        compiler_params=pltpu.CompilerParams(
+            collective_id=0, has_side_effects=True, vmem_limit_bytes=16 * 2**20
+        ),
+        name="gather_rows",
+    )(rows)
+
+
+def dot(a, b, left, right):
+    return lax.dot_general(
+        a, b, (((left,), (right,)), ((), ())), preferred_element_type=jnp.float32
+    )
+
+
+def padded(weight, enc_local):
+    gap = jnp.zeros((LANES - enc_local, weight.shape[1]), weight.dtype)
+    parts = []
+    for quarter in range(4):
+        parts += [weight[quarter * enc_local : (quarter + 1) * enc_local], gap]
+    return jnp.concatenate(parts, axis=0)
+
+
+def attend_kernel(group, counts_ref, slots_ref, rows_ref, q_ref, g_ref, wk_ref, wv_ref, att_ref, dq_ref, part_ref, grads, weights):
+    step = pl.program_id(0)
+    steps = pl.num_programs(0)
+    total_rows = rows_ref.shape[1]
+    enc_local = wk_ref.shape[0] // 4
+    tokens = q_ref.shape[0]
+    factor = 1.0 / HDIM**0.5
+    slot = lax.broadcasted_iota(jnp.int32, (SLOTS, tokens), 0)
+    span = lax.broadcasted_iota(jnp.int32, (SLOTS, tokens), 1) // SPAN
+    bias = jnp.full((SLOTS, tokens), -jnp.inf, jnp.float32)
+    for c in range(CH_DEV):
+        for j in range(MAX_NB):
+            wanted = jnp.where(j < counts_ref[c], slots_ref[0, c * MAX_NB + j], -1)
+            bias = jnp.where((slot == wanted) & (span == c), 0.0, bias)
+    rows = jnp.concatenate([rows_ref[quarter] for quarter in range(4)], axis=1)
+    blank = jnp.zeros((tokens, HDIM), jnp.bfloat16)
+    for i in range(group):
+        cut = slice(i * HDIM, (i + 1) * HDIM)
+        weight = padded(
+            jnp.concatenate([wk_ref[:, cut], wv_ref[:, cut]], axis=1), enc_local
+        )
+        weights[step * group + i] = weight
+        both = dot(rows, weight, 1, 0)
+        keys = both[:, :HDIM]
+        keys_high = keys.astype(jnp.bfloat16)
+        keys_low = (keys - keys_high.astype(jnp.float32)).astype(jnp.bfloat16)
+        split = jnp.concatenate([keys_high, keys_low], axis=1)
+        values = both[:, HDIM:].astype(jnp.bfloat16)
+        q = q_ref[:, cut]
+        g = g_ref[:, cut]
+        scores = dot(split, jnp.concatenate([q, q], axis=1), 1, 1)
+        scores = scores.reshape(total_rows // SLOTS, SLOTS, tokens)
+        scores = scores * (factor * math.log2(math.e)) + bias[None]
+        top = jnp.max(jnp.max(scores, axis=0), axis=0, keepdims=True)
+        expo = jnp.exp2(scores - top[None])
+        total = jnp.sum(jnp.sum(expo, axis=0), axis=0, keepdims=True)
+        probs = expo * (1.0 / total)[None]
+        dprobs = dot(values, g, 1, 1).reshape(probs.shape)
+        inner = jnp.sum(jnp.sum(probs * dprobs, axis=0), axis=0, keepdims=True)
+        dscores = (probs * (dprobs - inner[None])).reshape(total_rows, tokens)
+        dscores = dscores.astype(jnp.bfloat16)
+        probs_b = probs.reshape(total_rows, tokens).astype(jnp.bfloat16)
+        att_ref[:, cut] = dot(probs_b, values, 0, 0).astype(jnp.bfloat16)
+        dq = dot(dscores, split, 0, 0)
+        dq_ref[:, cut] = ((dq[:, :HDIM] + dq[:, HDIM:]) * factor).astype(jnp.bfloat16)
+        sources = jnp.concatenate(
+            [jnp.concatenate([q, blank], axis=1), jnp.concatenate([blank, g], axis=1)], axis=0
+        )
+        pair = dot(jnp.concatenate([dscores, probs_b], axis=1), sources, 1, 0)
+        grads[step * group + i, :, :HDIM] = (pair[:, :HDIM] * factor).astype(jnp.bfloat16)
+        grads[step * group + i, :, HDIM:] = pair[:, HDIM:].astype(jnp.bfloat16)
+
+    @pl.when(step == steps - 1)
+    def _():
+        heads = grads.shape[0]
+        chunk = 256
+
+        @pl.loop(0, total_rows // chunk)
+        def _(r):
+            here = pl.ds(pl.multiple_of(r * chunk, chunk), chunk)
+            total = dot(grads[0, here, :], weights[0], 1, 1)
+            for i in range(1, heads):
+                total = total + dot(grads[i, here, :], weights[i], 1, 1)
+            total = total.astype(jnp.bfloat16)
+            for quarter in range(4):
+                part_ref[quarter, here, :] = total[:, quarter * LANES : (quarter + 1) * LANES]
+
+
+def attend(group, counts, slot_map, rows, queries, grads, key_weight, value_weight):
+    tokens, width = queries.shape
+    enc = key_weight.shape[0]
+    total_rows = rows.shape[1]
+    heads = width // HDIM
+    wide = group * HDIM
+    column = lambda i: (0, i)
+    return pl.pallas_call(
+        functools.partial(attend_kernel, group),
+        grid=(heads // group,),
+        out_shape=[
+            jax.ShapeDtypeStruct((tokens, width), jnp.bfloat16),
+            jax.ShapeDtypeStruct((tokens, width), jnp.bfloat16),
+            jax.ShapeDtypeStruct((4, total_rows, LANES), jnp.bfloat16),
+        ],
+        in_specs=[
+            pl.BlockSpec(memory_space=pltpu.SMEM),
+            pl.BlockSpec(memory_space=pltpu.SMEM),
+            pl.BlockSpec((4, total_rows, LANES), lambda i: (0, 0, 0)),
+            pl.BlockSpec((tokens, wide), column),
+            pl.BlockSpec((tokens, wide), column),
+            pl.BlockSpec((enc, wide), column),
+            pl.BlockSpec((enc, wide), column),
+        ],
+        out_specs=[
+            pl.BlockSpec((tokens, wide), column),
+            pl.BlockSpec((tokens, wide), column),
+            pl.BlockSpec((4, total_rows, LANES), lambda i: (0, 0, 0)),
+        ],
+        scratch_shapes=[
+            pltpu.VMEM((heads, total_rows, 2 * HDIM), jnp.bfloat16),
+            pltpu.VMEM((heads, 4 * LANES, 2 * HDIM), jnp.bfloat16),
+        ],
+        compiler_params=pltpu.CompilerParams(vmem_limit_bytes=48 * 2**20),
+        name="attend_heads",
+    )(counts, slot_map, rows, queries, grads, key_weight, value_weight)
+
+
+def reduce_kernel(n_seq, block, part_ref, out_ref, a_buf, y_out, y_buf, done, a_send, a_recv, y_send, y_recv, s_send, s_recv):
+    me, head, y, core, across, beside = positions(n_seq)
+    greet(n_seq, me, head, across, beside)
+
+    def rows_of(owner):
+        return pl.ds(pl.multiple_of(owner * block, block), block)
+
+    order = list(range(n_seq - 1, -1, -1))
+    firsts = {}
+    for k in order:
+        owner = (me + k) % n_seq
+        for row in (0, 1):
+            copy = pltpu.make_async_remote_copy(
+                src_ref=part_ref.at[row * CORES + 1 - core, rows_of(owner), :],
+                dst_ref=a_buf.at[k, row],
+                send_sem=a_send.at[k, row],
+                recv_sem=a_recv.at[k, row],
+                device_id=(me, beside),
+                device_id_type=MESH_ID,
+            )
+            copy.start()
+            firsts[k, row] = copy
+    seconds = {}
+    for k in order:
+        owner = (me + k) % n_seq
+        for row in (0, 1):
+            firsts[k, row].wait_recv()
+        mixed = part_ref[across, rows_of(owner), :].astype(jnp.float32) + a_buf[k, 1 - y].astype(jnp.float32)
+        y_out[k] = mixed.astype(jnp.bfloat16)
+        copy = pltpu.make_async_remote_copy(
+            src_ref=y_out.at[k],
+            dst_ref=y_buf.at[k],
+            send_sem=y_send.at[k],
+            recv_sem=y_recv.at[k],
+            device_id=(me, across),
+            device_id_type=MESH_ID,
+        )
+        copy.start()
+        seconds[k] = copy
+    thirds = {}
+    for k in order:
+        owner = (me + k) % n_seq
+        seconds[k].wait_recv()
+        total = (
+            part_ref[head, rows_of(owner), :].astype(jnp.float32)
+            + a_buf[k, y].astype(jnp.float32)
+            + y_buf[k].astype(jnp.float32)
+        ).astype(jnp.bfloat16)
+        if k == 0:
+            out_ref[me] = total
+        else:
+            done[k] = total
+            copy = pltpu.make_async_remote_copy(
+                src_ref=done.at[k],
+                dst_ref=out_ref.at[me],
+                send_sem=s_send.at[k],
+                recv_sem=s_recv.at[k],
+                device_id=(owner, head),
+                device_id_type=MESH_ID,
+            )
+            copy.start()
+            thirds[k] = copy
+    for copy in thirds.values():
+        copy.wait_recv()
+    for copies in (firsts, seconds, thirds):
+        for copy in copies.values():
+            copy.wait_send()
+
+
+def reduce_back(n_seq, block, partial):
+    dma = pltpu.SemaphoreType.DMA
+    tile = (block, LANES)
+    return pl.pallas_call(
+        functools.partial(reduce_kernel, n_seq, block),
+        out_shape=jax.ShapeDtypeStruct((n_seq,) + tile, jnp.bfloat16),
+        in_specs=[pl.BlockSpec(memory_space=VMEM)],
+        out_specs=pl.BlockSpec(memory_space=VMEM),
+        scratch_shapes=[
+            pltpu.VMEM((n_seq, 2) + tile, jnp.bfloat16),
+            pltpu.VMEM((n_seq,) + tile, jnp.bfloat16),
+            pltpu.VMEM((n_seq,) + tile, jnp.bfloat16),
+            pltpu.VMEM((n_seq,) + tile, jnp.bfloat16),
+            dma((n_seq, 2)),
+            dma((n_seq, 2)),
+            dma((n_seq,)),
+            dma((n_seq,)),
+            dma((n_seq,)),
+            dma((n_seq,)),
+        ],
+        compiler_params=pltpu.CompilerParams(
+            collective_id=1, has_side_effects=True, vmem_limit_bytes=16 * 2**20
+        ),
+        name="reduce_rows",
+    )(partial)
+
+
+def per_device_kernels(n_seq, queries, neighbours, key_weight, value_weight, counts, slot_map, d_attended):
+    positions_local = neighbours.shape[1]
+    enc_local = neighbours.shape[3]
+    block = positions_local * SLOTS
+    rows = gather(n_seq, block, neighbours.reshape(n_seq * block, enc_local))
+    attended, d_queries, partial = attend(
+        2, counts, slot_map, rows, queries, d_attended, key_weight, value_weight
+    )
+    back = reduce_back(n_seq, block, partial)
+    d_neighbours = back[:, :, :enc_local].reshape(neighbours.shape)
+    return (attended, d_queries, d_neighbours)
+
+
 def solution(mesh):
+    n_seq, n_head = mesh.shape["seq"], mesh.shape["head"]
+    block = NB_LEN * SLOTS // n_seq
+    per_device = per_device_plain
+    if n_head == 4 and block % 32 == 0:
+        per_device = functools.partial(per_device_kernels, n_seq)
     in_specs = (
         P("seq", "head"),
         P(None, "seq", None, "head"),

time: 118 us -> 54.6 us (0.46)
  Pallas kernels: 0 us -> 49.8 us
  waiting for transfers between devices: 37.3 us -> 0 us
  matrix products: 25.6 us -> 0 us
  between operations: 14.2 us -> 0.71 us
  starting transfers between devices: 12.9 us -> 0 us
  blocking collectives: 9.34 us -> 0 us
  local copies, waits for them, and re-layouts: 12.4 us -> 3.88 us
  other arithmetic: 5.63 us -> 0 us
    pallas_call x0 -> x3, Pallas kernels: none -> 49.8 us  [the longest x1 18.6 us: gather(): pl.pallas_call(functools.partial(gather_kernel, n_seq, block), out_shape=...]
    psum x1 -> x0, waiting for transfers between devices: 33.8 us -> none  [per_device(): lax.psum(partial_value.astype(jnp.bfloat16), 'head').astype(jnp.float32)]
    dot_general x10 -> x0, matrix products: 25.6 us -> none  [the longest x1 4.31 us: per_device(): jnp.einsum('htr,rhd->thd', dscores.astype(jnp.float32), keys, precision=h...]
    all_to_all x2 -> x0, starting transfers between devices: 12.9 us -> none  [the longest x1 7.4 us: per_device(): lax.all_to_all(neighbours, 'seq', split_axis=0, concat_axis=1, tiled=True)]
    all_gather x1 -> x0, blocking collectives: 9.34 us -> none  [per_device(): portion = lax.all_gather(flat_rows, 'head', axis=1, tiled=True)]
    convert_element_type x2 -> x0, local copies, waits for them, and re-layouts: 4.75 us -> none  [the longest x1 3.91 us: per_device(): d_keys = d_keys.astype(jnp.bfloat16).reshape(total_rows, width_local)]
    all_to_all x2 -> x0, waiting for transfers between devices: 3.57 us -> none  [the longest x1 3.57 us: per_device(): lax.all_to_all(neighbours, 'seq', split_axis=0, concat_axis=1, tiled=True)]
    sub x1 -> x0, other arithmetic: 1.94 us -> none  [per_device(): expo = jnp.exp(scores - top)]
  transfers between devices with their start and end apart: 3 -> 0, of which waited for: 2 -> 0; matrix products, arithmetic and copies ran while one was open for 13% -> 0% of each run, Pallas kernels for 0% -> 0%
where the time goes in v1:
time: 54.6 us; the launch traced here: 54.4 us
  Pallas kernels  49.8 us (91%)
  local copies, waits for them, and re-layouts  3.88 us (7%)
  between operations  0.71 us (1%)
    pallas_call x1, Pallas kernels, gather(): pl.pallas_call(functools.partial(gather_kernel, n_seq, block), out_shape=...  18.6 us
    pallas_call x1, Pallas kernels, attend(): pl.pallas_call(functools.partial(attend_kernel, group), grid=(heads // gr...  16 us
    pallas_call x1, Pallas kernels, reduce_back(): pl.pallas_call(functools.partial(reduce_kernel, n_seq, block), out_shape=...  15.2 us
    unnamed x14, local copies, waits for them, and re-layouts  3.16 us

profile of v1, /device:TPU:0, one launch (start us, length us, event | category | flops | bytes accessed | tf_op | source)
XLA Modules:
  0.0 54.4 jit_solution(15416036891606579106)
XLA Ops:
  0.6 0.0 copy-start
  0.6 0.0 copy-start.2
  0.7 1.0 %copy-done.2 = bf16[8,16,8,112]{3,2,1,0:T(8,128)(2,1)S(1)} copy-done((bf16[8,16,8,112]{3,2,1,0:T(8,128)(2,1)S(1)}, bf16[8,16,8,112]{3,2,1,0:T(8,128)(2,1)}, u32[]{:S(2)}) %copy-start.2) | copy-done | bytes 229400
  1.7 0.0 copy-start.3
  1.7 0.0 copy-start.5
  1.7 0.0 copy-start.6
  1.7 18.6 %gather_rows.1.rows_ref = bf16[4,1024,128]{2,1,0:T(8,128)(2,1)S(1)} custom-call(bf16[1024,112]{1,0:T(8,128)(2,1)S(1)} %bitcast.3), custom_call_target="tpu_custom_call" | custom-call | tf_op jit(solution)/shard_map/gather_rows/pallas_call | solution.py:196
  20.3 0.0 copy-done
  20.3 0.0 copy-done.3
  20.3 0.0 copy-done.5
  20.3 0.0 copy-done.6
  20.3 0.0 copy-start.1
  20.3 1.2 %copy-done.1 = bf16[448,1024]{1,0:T(8,128)(2,1)S(1)} copy-done((bf16[448,1024]{1,0:T(8,128)(2,1)S(1)}, bf16[448,1024]{1,0:T(8,128)(2,1)}, u32[]{:S(2)}) %copy-start.1) | copy-done | bytes 917528
  21.5 0.0 copy-start.4
  21.5 0.9 %copy-done.4 = bf16[128,1024]{1,0:T(8,128)(2,1)S(1)} copy-done((bf16[128,1024]{1,0:T(8,128)(2,1)S(1)}, bf16[128,1024]{1,0:T(8,128)(2,1)}, u32[]{:S(2)}) %copy-start.4) | copy-done | bytes 262168
  22.5 16.0 %attend_heads.1 = (bf16[128,1024]{1,0:T(8,128)(2,1)}, bf16[128,1024]{1,0:T(8,128)(2,1)}, bf16[4,1024,128]{2,1,0:T(8,128)(2,1)S(1)}) custom-call(s32[2]{0:T(128)S(1)} %copy-done.5, s32[1,8]{1,0:T(1,128)S(1)} %copy-done.6, bf16[4,1024,128]{2,1,0:T(8,128)(2,1)S(1)} %gather_rows.1.rows_ref, bf16[128,1024]{1,0:T(8,128)(2,1)S(1)} %copy-done.3, ...), custom_call_target="tpu_custom_call" | custom-call | tf_op jit(solution)/shard_map/attend_heads/pallas_call | solution.py:299
  38.5 15.2 %reduce_rows.1 = bf16[8,128,128]{2,1,0:T(8,128)(2,1)S(1)} custom-call(bf16[4,1024,128]{2,1,0:T(8,128)(2,1)S(1)} %get-tuple-element.8.part_ref), custom_call_target="tpu_custom_call" | custom-call | tf_op jit(solution)/shard_map/reduce_rows/pallas_call | solution.py:402
  53.7 0.7 %slice_bitcast_fusion = bf16[8,16,8,112]{3,2,1,0:T(8,128)(2,1)} fusion(bf16[8,128,128]{2,1,0:T(8,128)(2,1)S(1)} %reduce_rows.1), kind=kLoop, calls=%fused_computation | loop fusion | bytes 458752 | tf_op jit(solution)/shard_map/reshape | solution.py:435
Async XLA Ops:
  0.6 19.7 %copy-start = (bf16[448,1024]{1,0:T(8,128)(2,1)S(1)}, bf16[448,1024]{1,0:T(8,128)(2,1)}, u32[]{:S(2)}) copy-start(bf16[448,1024]{1,0:T(8,128)(2,1)} %wk_ref.1) | copy-start | bytes 2752516
  0.6 1.0 %copy-start.2 = (bf16[8,16,8,112]{3,2,1,0:T(8,128)(2,1)S(1)}, bf16[8,16,8,112]{3,2,1,0:T(8,128)(2,1)}, u32[]{:S(2)}) copy-start(bf16[8,16,8,112]{3,2,1,0:T(8,128)(2,1)} %param.8) | copy-start | bytes 688132
  1.7 18.6 %copy-start.3 = (bf16[128,1024]{1,0:T(8,128)(2,1)S(1)}, bf16[128,1024]{1,0:T(8,128)(2,1)}, u32[]{:S(2)}) copy-start(bf16[128,1024]{1,0:T(8,128)(2,1)} %q_ref.1) | copy-start | bytes 786436
  1.7 18.6 %copy-start.5 = (s32[2]{0:T(128)S(1)}, s32[2]{0:T(128)}, u32[]{:S(2)}) copy-start(s32[2]{0:T(128)} %counts_ref.1) | copy-start | bytes 28
  1.7 18.6 %copy-start.6 = (s32[1,8]{1,0:T(1,128)S(1)}, s32[1,8]{1,0:T(1,128)}, u32[]{:S(2)}) copy-start(s32[1,8]{1,0:T(1,128)} %slots_ref.1) | copy-start | bytes 100
  20.3 1.2 %copy-start.1 = (bf16[448,1024]{1,0:T(8,128)(2,1)S(1)}, bf16[448,1024]{1,0:T(8,128)(2,1)}, u32[]{:S(2)}) copy-start(bf16[448,1024]{1,0:T(8,128)(2,1)} %wv_ref.1) | copy-start | bytes 2752516
  21.5 0.9 %copy-start.4 = (bf16[128,1024]{1,0:T(8,128)(2,1)S(1)}, bf16[128,1024]{1,0:T(8,128)(2,1)}, u32[]{:S(2)}) copy-start(bf16[128,1024]{1,0:T(8,128)(2,1)} %g_ref.1) | copy-start | bytes 786436

commit v2 on v1

--- a/solution.py
+++ b/solution.py
@@ -121,15 +121,12 @@
     pl.semaphore_wait(barrier, n_seq + 1)
 
 
-def gather_kernel(n_seq, block, nb_ref, rows_ref, packed, own_sem, s_send, s_recv, y_send, y_recv, c_send, c_recv, f_send, f_recv):
+def gather_kernel(n_seq, block, nb_ref, rows_ref, own_sem, s_send, s_recv, y_send, y_recv, c_send, c_recv, f_send, f_recv):
     me, head, y, core, across, beside = positions(n_seq)
-    enc_local = nb_ref.shape[1]
-    packed[...] = jnp.zeros_like(packed)
-    packed[:, :enc_local] = nb_ref[...]
     greet(n_seq, me, head, across, beside)
 
     def rows_of(quarter, owner):
-        return rows_ref.at[quarter, pl.ds(pl.multiple_of(owner * block, block), block), :]
+        return rows_ref.at[quarter, :, pl.ds(pl.multiple_of(owner * block, block), block), :]
 
     def remote(src, dst, send, recv, device):
         return pltpu.make_async_remote_copy(
@@ -142,14 +139,14 @@
         )
 
     own = pltpu.make_async_copy(
-        packed.at[pl.ds(pl.multiple_of(me * block, block), block), :], rows_of(head, me), own_sem
+        nb_ref.at[me], rows_of(head, me), own_sem
     )
     own.start()
     sent = []
     for k in range(n_seq - 1, 0, -1):
         to = (me + k) % n_seq
         copy = remote(
-            packed.at[pl.ds(pl.multiple_of(to * block, block), block), :],
+            nb_ref.at[to],
             rows_of(head, me),
             s_send.at[k],
             s_recv.at[k],
@@ -195,14 +192,14 @@
     dma = pltpu.SemaphoreType.DMA
     return pl.pallas_call(
         functools.partial(gather_kernel, n_seq, block),
-        out_shape=jax.ShapeDtypeStruct((4, n_seq * block, LANES), jnp.bfloat16),
+        out_shape=jax.ShapeDtypeStruct((4, SLOTS, n_seq * block, LANES), jnp.bfloat16),
         in_specs=[pl.BlockSpec(memory_space=VMEM)],
         out_specs=pl.BlockSpec(memory_space=VMEM),
-        scratch_shapes=[pltpu.VMEM((n_seq * block, LANES), jnp.bfloat16), dma]
-        + [dma((n_seq,)) for _ in range(8)],
+        scratch_shapes=[dma] + [dma((n_seq,)) for _ in range(8)],
         compiler_params=pltpu.CompilerParams(
             collective_id=0, has_side_effects=True, vmem_limit_bytes=16 * 2**20
         ),
+        cost_estimate=pl.CostEstimate(flops=0, bytes_accessed=40 * 2**20, transcendentals=0),
         name="gather_rows",
     )(rows)
 
@@ -224,19 +221,40 @@
 def attend_kernel(group, counts_ref, slots_ref, rows_ref, q_ref, g_ref, wk_ref, wv_ref, att_ref, dq_ref, part_ref, grads, weights):
     step = pl.program_id(0)
     steps = pl.num_programs(0)
-    total_rows = rows_ref.shape[1]
+    length = rows_ref.shape[2]
+    half = MAX_NB * length
     enc_local = wk_ref.shape[0] // 4
     tokens = q_ref.shape[0]
     factor = 1.0 / HDIM**0.5
-    slot = lax.broadcasted_iota(jnp.int32, (SLOTS, tokens), 0)
-    span = lax.broadcasted_iota(jnp.int32, (SLOTS, tokens), 1) // SPAN
-    bias = jnp.full((SLOTS, tokens), -jnp.inf, jnp.float32)
-    for c in range(CH_DEV):
-        for j in range(MAX_NB):
-            wanted = jnp.where(j < counts_ref[c], slots_ref[0, c * MAX_NB + j], -1)
-            bias = jnp.where((slot == wanted) & (span == c), 0.0, bias)
-    rows = jnp.concatenate([rows_ref[quarter] for quarter in range(4)], axis=1)
-    blank = jnp.zeros((tokens, HDIM), jnp.bfloat16)
+    late = lax.broadcasted_iota(jnp.int32, (1, tokens), 1) >= SPAN
+    own_count = jnp.where(late, counts_ref[1], counts_ref[0])
+    bias = [jnp.where(j < own_count, 0.0, -jnp.inf)[None] for j in range(MAX_NB)]
+    bias = jnp.concatenate(bias, axis=0)
+    slots = [slots_ref[0, i] for i in range(SLOTS)]
+    rows = jnp.concatenate(
+        [
+            jnp.concatenate([rows_ref[quarter, slots[i]] for quarter in range(4)], axis=1)
+            for i in range(SLOTS)
+        ],
+        axis=0,
+    )
+    blank = jnp.zeros((SPAN, HDIM), jnp.bfloat16)
+
+    def spread(x):
+        return jnp.concatenate(
+            [
+                jnp.concatenate([x[:SPAN], blank], axis=1),
+                jnp.concatenate([blank, x[SPAN:]], axis=1),
+            ],
+            axis=0,
+        )
+
+    def beside_each_other(x):
+        return jnp.concatenate([x[:half], x[half:]], axis=1)
+
+    def diagonal(x):
+        return jnp.concatenate([x[:SPAN, :HDIM], x[SPAN:, HDIM:]], axis=0)
+
     for i in range(group):
         cut = slice(i * HDIM, (i + 1) * HDIM)
         weight = padded(
@@ -244,56 +262,61 @@
         )
         weights[step * group + i] = weight
         both = dot(rows, weight, 1, 0)
-        keys = both[:, :HDIM]
+        keys = beside_each_other(both[:, :HDIM])
         keys_high = keys.astype(jnp.bfloat16)
         keys_low = (keys - keys_high.astype(jnp.float32)).astype(jnp.bfloat16)
-        split = jnp.concatenate([keys_high, keys_low], axis=1)
-        values = both[:, HDIM:].astype(jnp.bfloat16)
-        q = q_ref[:, cut]
-        g = g_ref[:, cut]
-        scores = dot(split, jnp.concatenate([q, q], axis=1), 1, 1)
-        scores = scores.reshape(total_rows // SLOTS, SLOTS, tokens)
-        scores = scores * (factor * math.log2(math.e)) + bias[None]
+        values = beside_each_other(both[:, HDIM:]).astype(jnp.bfloat16)
+        q = spread(q_ref[:, cut])
+        g = spread(g_ref[:, cut])
+        scores = dot(keys_high, q, 1, 1) + dot(keys_low, q, 1, 1)
+        scores = scores.reshape(MAX_NB, length, tokens)
+        scores = scores * (factor * math.log2(math.e)) + bias
         top = jnp.max(jnp.max(scores, axis=0), axis=0, keepdims=True)
         expo = jnp.exp2(scores - top[None])
         total = jnp.sum(jnp.sum(expo, axis=0), axis=0, keepdims=True)
         probs = expo * (1.0 / total)[None]
         dprobs = dot(values, g, 1, 1).reshape(probs.shape)
         inner = jnp.sum(jnp.sum(probs * dprobs, axis=0), axis=0, keepdims=True)
-        dscores = (probs * (dprobs - inner[None])).reshape(total_rows, tokens)
+        dscores = (probs * (dprobs - inner[None])).reshape(half, tokens)
         dscores = dscores.astype(jnp.bfloat16)
-        probs_b = probs.reshape(total_rows, tokens).astype(jnp.bfloat16)
-        att_ref[:, cut] = dot(probs_b, values, 0, 0).astype(jnp.bfloat16)
-        dq = dot(dscores, split, 0, 0)
-        dq_ref[:, cut] = ((dq[:, :HDIM] + dq[:, HDIM:]) * factor).astype(jnp.bfloat16)
-        sources = jnp.concatenate(
-            [jnp.concatenate([q, blank], axis=1), jnp.concatenate([blank, g], axis=1)], axis=0
-        )
-        pair = dot(jnp.concatenate([dscores, probs_b], axis=1), sources, 1, 0)
-        grads[step * group + i, :, :HDIM] = (pair[:, :HDIM] * factor).astype(jnp.bfloat16)
-        grads[step * group + i, :, HDIM:] = pair[:, HDIM:].astype(jnp.bfloat16)
+        probs_b = probs.reshape(half, tokens).astype(jnp.bfloat16)
+        att_ref[:, cut] = diagonal(dot(probs_b, values, 0, 0)).astype(jnp.bfloat16)
+        dq = diagonal(dot(dscores, keys_high, 0, 0) + dot(dscores, keys_low, 0, 0))
+        dq_ref[:, cut] = (dq * factor).astype(jnp.bfloat16)
+        d_keys = (dot(dscores, q, 1, 0) * factor).astype(jnp.bfloat16)
+        d_values = dot(probs_b, g, 1, 0).astype(jnp.bfloat16)
+        for c in range(CH_DEV):
+            part = slice(c * half, (c + 1) * half)
+            side = slice(c * HDIM, (c + 1) * HDIM)
+            grads[step * group + i, part, :HDIM] = d_keys[:, side]
+            grads[step * group + i, part, HDIM:] = d_values[:, side]
 
     @pl.when(step == steps - 1)
     def _():
         heads = grads.shape[0]
-        chunk = 256
-
-        @pl.loop(0, total_rows // chunk)
+        chunk = 2 * length
+
+        @pl.loop(0, SLOTS // 2)
         def _(r):
             here = pl.ds(pl.multiple_of(r * chunk, chunk), chunk)
             total = dot(grads[0, here, :], weights[0], 1, 1)
             for i in range(1, heads):
                 total = total + dot(grads[i, here, :], weights[i], 1, 1)
             total = total.astype(jnp.bfloat16)
-            for quarter in range(4):
-                part_ref[quarter, here, :] = total[:, quarter * LANES : (quarter + 1) * LANES]
+            for row in range(2):
+                slot = slots_ref[0, 2 * r + row]
+                for quarter in range(4):
+                    part_ref[quarter, slot] = total[
+                        row * length : (row + 1) * length, quarter * LANES : (quarter + 1) * LANES
+                    ]
 
 
 def attend(group, counts, slot_map, rows, queries, grads, key_weight, value_weight):
     tokens, width = queries.shape
     enc = key_weight.shape[0]
-    total_rows = rows.shape[1]
+    length = rows.shape[2]
     heads = width // HDIM
+    whole = (4, SLOTS, length, LANES)
     wide = group * HDIM
     column = lambda i: (0, i)
     return pl.pallas_call(
@@ -302,12 +325,12 @@
         out_shape=[
             jax.ShapeDtypeStruct((tokens, width), jnp.bfloat16),
             jax.ShapeDtypeStruct((tokens, width), jnp.bfloat16),
-            jax.ShapeDtypeStruct((4, total_rows, LANES), jnp.bfloat16),
+            jax.ShapeDtypeStruct(whole, jnp.bfloat16),
         ],
         in_specs=[
             pl.BlockSpec(memory_space=pltpu.SMEM),
             pl.BlockSpec(memory_space=pltpu.SMEM),
-            pl.BlockSpec((4, total_rows, LANES), lambda i: (0, 0, 0)),
+            pl.BlockSpec(whole, lambda i: (0, 0, 0, 0)),
             pl.BlockSpec((tokens, wide), column),
             pl.BlockSpec((tokens, wide), column),
             pl.BlockSpec((enc, wide), column),
@@ -316,10 +339,10 @@
         out_specs=[
             pl.BlockSpec((tokens, wide), column),
             pl.BlockSpec((tokens, wide), column),
-            pl.BlockSpec((4, total_rows, LANES), lambda i: (0, 0, 0)),
+            pl.BlockSpec(whole, lambda i: (0, 0, 0, 0)),
         ],
         scratch_shapes=[
-            pltpu.VMEM((heads, total_rows, 2 * HDIM), jnp.bfloat16),
+            pltpu.VMEM((heads, SLOTS * length, 2 * HDIM), jnp.bfloat16),
             pltpu.VMEM((heads, 4 * LANES, 2 * HDIM), jnp.bfloat16),
         ],
         compiler_params=pltpu.CompilerParams(vmem_limit_bytes=48 * 2**20),
@@ -340,7 +363,7 @@
         owner = (me + k) % n_seq
         for row in (0, 1):
             copy = pltpu.make_async_remote_copy(
-                src_ref=part_ref.at[row * CORES + 1 - core, rows_of(owner), :],
+                src_ref=part_ref.at[row * CORES + 1 - core, :, rows_of(owner), :],
                 dst_ref=a_buf.at[k, row],
                 send_sem=a_send.at[k, row],
                 recv_sem=a_recv.at[k, row],
@@ -354,7 +377,7 @@
         owner = (me + k) % n_seq
         for row in (0, 1):
             firsts[k, row].wait_recv()
-        mixed = part_ref[across, rows_of(owner), :].astype(jnp.float32) + a_buf[k, 1 - y].astype(jnp.float32)
+        mixed = part_ref[across, :, rows_of(owner), :].astype(jnp.float32) + a_buf[k, 1 - y].astype(jnp.float32)
         y_out[k] = mixed.astype(jnp.bfloat16)
         copy = pltpu.make_async_remote_copy(
             src_ref=y_out.at[k],
@@ -371,7 +394,7 @@
         owner = (me + k) % n_seq
         seconds[k].wait_recv()
         total = (
-            part_ref[head, rows_of(owner), :].astype(jnp.float32)
+            part_ref[head, :, rows_of(owner), :].astype(jnp.float32)
             + a_buf[k, y].astype(jnp.float32)
             + y_buf[k].astype(jnp.float32)
         ).astype(jnp.bfloat16)
@@ -398,7 +421,7 @@
 
 def reduce_back(n_seq, block, partial):
     dma = pltpu.SemaphoreType.DMA
-    tile = (block, LANES)
+    tile = (SLOTS, block, LANES)
     return pl.pallas_call(
         functools.partial(reduce_kernel, n_seq, block),
         out_shape=jax.ShapeDtypeStruct((n_seq,) + tile, jnp.bfloat16),
@@ -424,23 +447,25 @@
 
 
 def per_device_kernels(n_seq, queries, neighbours, key_weight, value_weight, counts, slot_map, d_attended):
-    positions_local = neighbours.shape[1]
+    block = neighbours.shape[1]
     enc_local = neighbours.shape[3]
-    block = positions_local * SLOTS
-    rows = gather(n_seq, block, neighbours.reshape(n_seq * block, enc_local))
+    by_slot = jnp.pad(
+        neighbours.transpose(0, 2, 1, 3), ((0, 0), (0, 0), (0, 0), (0, LANES - enc_local))
+    )
+    rows = gather(n_seq, block, by_slot)
     attended, d_queries, partial = attend(
         2, counts, slot_map, rows, queries, d_attended, key_weight, value_weight
     )
     back = reduce_back(n_seq, block, partial)
-    d_neighbours = back[:, :, :enc_local].reshape(neighbours.shape)
+    d_neighbours = back[:, :, :, :enc_local].transpose(0, 2, 1, 3)
     return (attended, d_queries, d_neighbours)
 
 
 def solution(mesh):
     n_seq, n_head = mesh.shape["seq"], mesh.shape["head"]
-    block = NB_LEN * SLOTS // n_seq
+    block = NB_LEN // n_seq
     per_device = per_device_plain
-    if n_head == 4 and block % 32 == 0:
+    if n_head == 4 and block % 16 == 0:
         per_device = functools.partial(per_device_kernels, n_seq)
     in_specs = (
         P("seq", "head"),

time: 54.6 us -> 52.2 us (0.956)
  local copies, waits for them, and re-layouts: 3.88 us -> 1.92 us
    unnamed x14, local copies, waits for them, and re-layouts: 3.16 us -> 1.84 us
    reshape x1 -> x0, local copies, waits for them, and re-layouts: 0.72 us -> none  [per_device_kernels(): d_neighbours = back[:, :, :enc_local].reshape(neighbours.shape)]
where the time goes in v2:
time: 52.2 us; the launch traced here: 52 us
  Pallas kernels  49.3 us (94%)
  local copies, waits for them, and re-layouts  1.92 us (4%)
  between operations  0.77 us (1%)
    pallas_call x1, Pallas kernels, gather(): pl.pallas_call(functools.partial(gather_kernel, n_seq, block), out_shape=...  18.6 us
    pallas_call x1, Pallas kernels, attend(): pl.pallas_call(functools.partial(attend_kernel, group), grid=(heads // gr...  15.5 us
    pallas_call x1, Pallas kernels, reduce_back(): pl.pallas_call(functools.partial(reduce_kernel, n_seq, block), out_shape=...  15.3 us
    unnamed x14, local copies, waits for them, and re-layouts  1.84 us

profile of v2, /device:TPU:0, one launch (start us, length us, event | category | flops | bytes accessed | tf_op | source)
XLA Modules:
  0.0 52.0 jit_solution(2952566812113522009)
XLA Ops:
  0.6 0.0 copy-start.2
  0.6 0.0 copy-start.3
  0.7 0.0 copy-start.5
  0.7 1.0 %copy.13 = bf16[8,16,8,112]{3,1,2,0:T(8,128)(2,1)S(1)} copy(bf16[8,16,8,112]{3,2,1,0:T(8,128)(2,1)} %param.8) | data formatting | bytes 458752 | tf_op args[1]
  1.7 0.0 copy-start
  1.7 0.0 copy-start.1
  1.7 0.1 pad.4.nb_ref
  1.8 0.0 copy-start.4
  1.8 18.6 %gather_rows.1.rows_ref = bf16[4,8,128,128]{3,2,1,0:T(8,128)(2,1)S(1)} custom-call(bf16[8,8,16,128]{3,2,1,0:T(8,128)(2,1)S(1)} %pad.4.nb_ref), custom_call_target="tpu_custom_call" | custom-call | bytes 41943040 | tf_op jit(solution)/shard_map/gather_rows/pallas_call | solution.py:193
  20.4 0.0 copy-done.2
  20.4 0.0 copy-done.3
  20.4 0.0 copy-done.5
  20.4 0.0 copy-done
  20.4 0.0 copy-done.1
  20.4 0.0 copy-done.4
  20.4 15.5 %attend_heads.1 = (bf16[128,1024]{1,0:T(8,128)(2,1)}, bf16[128,1024]{1,0:T(8,128)(2,1)}, bf16[4,8,128,128]{3,2,1,0:T(8,128)(2,1)S(1)}) custom-call(s32[2]{0:T(128)S(1)} %copy-done.4, s32[1,8]{1,0:T(1,128)S(1)} %copy-done.5, bf16[4,8,128,128]{3,2,1,0:T(8,128)(2,1)S(1)} %gather_rows.1.rows_ref, bf16[128,1024]{1,0:T(8,128)(2,1)S(1)} %copy-done.2, ...), custom_call_target="tpu_custom_call" | custom-call | tf_op jit(solution)/shard_map/attend_heads/pallas_call | solution.py:322
  36.0 15.3 %reduce_rows.1 = bf16[8,8,16,128]{3,2,1,0:T(8,128)(2,1)S(1)} custom-call(bf16[4,8,128,128]{3,2,1,0:T(8,128)(2,1)S(1)} %get-tuple-element.8.part_ref), custom_call_target="tpu_custom_call" | custom-call | tf_op jit(solution)/shard_map/reduce_rows/pallas_call | solution.py:425
  51.3 0.8 %copy.11 = bf16[8,16,8,112]{3,2,1,0:T(8,128)(2,1)} copy(bf16[8,16,8,112]{3,1,2,0:T(8,128)(2,1)S(1)} %slice_bitcast_fusion) | data formatting | bytes 458752
  (1 shorter events, 0.0 us)
Async XLA Ops:
  0.6 19.7 %copy-start.2 = (bf16[128,1024]{1,0:T(8,128)(2,1)S(1)}, bf16[128,1024]{1,0:T(8,128)(2,1)}, u32[]{:S(2)}) copy-start(bf16[128,1024]{1,0:T(8,128)(2,1)} %q_ref.1) | copy-start | bytes 786436
  0.6 19.7 %copy-start.3 = (bf16[128,1024]{1,0:T(8,128)(2,1)S(1)}, bf16[128,1024]{1,0:T(8,128)(2,1)}, u32[]{:S(2)}) copy-start(bf16[128,1024]{1,0:T(8,128)(2,1)} %g_ref.1) | copy-start | bytes 786436
  0.7 19.7 %copy-start.5 = (s32[1,8]{1,0:T(1,128)S(1)}, s32[1,8]{1,0:T(1,128)}, u32[]{:S(2)}) copy-start(s32[1,8]{1,0:T(1,128)} %slots_ref.1) | copy-start | bytes 100
  1.7 18.7 %copy-start = (bf16[448,1024]{1,0:T(8,128)(2,1)S(1)}, bf16[448,1024]{1,0:T(8,128)(2,1)}, u32[]{:S(2)}) copy-start(bf16[448,1024]{1,0:T(8,128)(2,1)} %wk_ref.1) | copy-start | bytes 2752516
  1.7 18.7 %copy-start.1 = (bf16[448,1024]{1,0:T(8,128)(2,1)S(1)}, bf16[448,1024]{1,0:T(8,128)(2,1)}, u32[]{:S(2)}) copy-start(bf16[448,1024]{1,0:T(8,128)(2,1)} %wv_ref.1) | copy-start | bytes 2752516
  1.8 18.6 %copy-start.4 = (s32[2]{0:T(128)S(1)}, s32[2]{0:T(128)}, u32[]{:S(2)}) copy-start(s32[2]{0:T(128)} %counts_ref.1) | copy-start | bytes 28

commit v3 on v2

--- a/solution.py
+++ b/solution.py
@@ -218,7 +218,7 @@
     return jnp.concatenate(parts, axis=0)
 
 
-def attend_kernel(group, counts_ref, slots_ref, rows_ref, q_ref, g_ref, wk_ref, wv_ref, att_ref, dq_ref, part_ref, grads, weights):
+def attend_kernel(group, counts_ref, slots_ref, rows_ref, q_ref, g_ref, wk_ref, wv_ref, att_ref, dq_ref, part_ref, grads, weights, rows):
     step = pl.program_id(0)
     steps = pl.num_programs(0)
     length = rows_ref.shape[2]
@@ -231,13 +231,15 @@
     bias = [jnp.where(j < own_count, 0.0, -jnp.inf)[None] for j in range(MAX_NB)]
     bias = jnp.concatenate(bias, axis=0)
     slots = [slots_ref[0, i] for i in range(SLOTS)]
-    rows = jnp.concatenate(
-        [
-            jnp.concatenate([rows_ref[quarter, slots[i]] for quarter in range(4)], axis=1)
-            for i in range(SLOTS)
-        ],
-        axis=0,
-    )
+
+    @pl.when(step == 0)
+    def _():
+        for i in range(SLOTS):
+            for quarter in range(4):
+                rows[
+                    i * length : (i + 1) * length, quarter * LANES : (quarter + 1) * LANES
+                ] = rows_ref[quarter, slots[i]]
+
     blank = jnp.zeros((SPAN, HDIM), jnp.bfloat16)
 
     def spread(x):
@@ -260,15 +262,18 @@
         weight = padded(
             jnp.concatenate([wk_ref[:, cut], wv_ref[:, cut]], axis=1), enc_local
         )
-        weights[step * group + i] = weight
-        both = dot(rows, weight, 1, 0)
+        head = step * group + i
+        lanes = pl.ds(pl.multiple_of(head * 2 * HDIM, 2 * HDIM), 2 * HDIM)
+        weights[:, lanes] = weight
+        both = dot(rows[...], weight, 1, 0)
         keys = beside_each_other(both[:, :HDIM])
         keys_high = keys.astype(jnp.bfloat16)
         keys_low = (keys - keys_high.astype(jnp.float32)).astype(jnp.bfloat16)
         values = beside_each_other(both[:, HDIM:]).astype(jnp.bfloat16)
         q = spread(q_ref[:, cut])
         g = spread(g_ref[:, cut])
-        scores = dot(keys_high, q, 1, 1) + dot(keys_low, q, 1, 1)
+        split = jnp.concatenate([keys_high, keys_low], axis=1)
+        scores = dot(split, jnp.concatenate([q, q], axis=1), 1, 1)
         scores = scores.reshape(MAX_NB, length, tokens)
         scores = scores * (factor * math.log2(math.e)) + bias
         top = jnp.max(jnp.max(scores, axis=0), axis=0, keepdims=True)
@@ -285,23 +290,22 @@
         dq_ref[:, cut] = (dq * factor).astype(jnp.bfloat16)
         d_keys = (dot(dscores, q, 1, 0) * factor).astype(jnp.bfloat16)
         d_values = dot(probs_b, g, 1, 0).astype(jnp.bfloat16)
-        for c in range(CH_DEV):
-            part = slice(c * half, (c + 1) * half)
-            side = slice(c * HDIM, (c + 1) * HDIM)
-            grads[step * group + i, part, :HDIM] = d_keys[:, side]
-            grads[step * group + i, part, HDIM:] = d_values[:, side]
+        pair = [
+            jnp.concatenate(
+                [d_keys[:, c * HDIM : (c + 1) * HDIM], d_values[:, c * HDIM : (c + 1) * HDIM]], axis=1
+            )
+            for c in range(CH_DEV)
+        ]
+        grads[:, lanes] = jnp.concatenate(pair, axis=0)
 
     @pl.when(step == steps - 1)
     def _():
-        heads = grads.shape[0]
         chunk = 2 * length
 
         @pl.loop(0, SLOTS // 2)
         def _(r):
             here = pl.ds(pl.multiple_of(r * chunk, chunk), chunk)
-            total = dot(grads[0, here, :], weights[0], 1, 1)
-            for i in range(1, heads):
-                total = total + dot(grads[i, here, :], weights[i], 1, 1)
+            total = dot(grads[here, :], weights[...], 1, 1)
             total = total.astype(jnp.bfloat16)
             for row in range(2):
                 slot = slots_ref[0, 2 * r + row]
@@ -342,8 +346,9 @@
             pl.BlockSpec(whole, lambda i: (0, 0, 0, 0)),
         ],
         scratch_shapes=[
-            pltpu.VMEM((heads, SLOTS * length, 2 * HDIM), jnp.bfloat16),
-            pltpu.VMEM((heads, 4 * LANES, 2 * HDIM), jnp.bfloat16),
+            pltpu.VMEM((SLOTS * length, 2 * width), jnp.bfloat16),
+            pltpu.VMEM((4 * LANES, 2 * width), jnp.bfloat16),
+            pltpu.VMEM((SLOTS * length, 4 * LANES), jnp.bfloat16),
         ],
         compiler_params=pltpu.CompilerParams(vmem_limit_bytes=48 * 2**20),
         name="attend_heads",
@@ -357,7 +362,7 @@
     def rows_of(owner):
         return pl.ds(pl.multiple_of(owner * block, block), block)
 
-    order = list(range(n_seq - 1, -1, -1))
+    order = sorted(range(n_seq), key=lambda k: -min(k, n_seq - k))
     firsts = {}
     for k in order:
         owner = (me + k) % n_seq

time: 52.2 us -> 51.6 us (0.989)
  Pallas kernels: 49.3 us -> 48.7 us
    pallas_call x1, Pallas kernels: 15.3 us -> 14.4 us  [reduce_back(): pl.pallas_call(functools.partial(reduce_kernel, n_seq, block), out_shape=...]
where the time goes in v3:
time: 51.6 us; the launch traced here: 51.4 us
  Pallas kernels  48.7 us (94%)
  local copies, waits for them, and re-layouts  1.92 us (4%)
  between operations  0.77 us (1%)
    pallas_call x1, Pallas kernels, gather(): pl.pallas_call(functools.partial(gather_kernel, n_seq, block), out_shape=...  18.6 us
    pallas_call x1, Pallas kernels, attend(): pl.pallas_call(functools.partial(attend_kernel, group), grid=(heads // gr...  15.8 us
    pallas_call x1, Pallas kernels, reduce_back(): pl.pallas_call(functools.partial(reduce_kernel, n_seq, block), out_shape=...  14.4 us
    unnamed x14, local copies, waits for them, and re-layouts  1.84 us

profile of v3, /device:TPU:0, one launch (start us, length us, event | category | flops | bytes accessed | tf_op | source)
XLA Modules:
  0.0 51.4 jit_solution(11744107139596321779)
XLA Ops:
  0.6 0.0 copy-start.2
  0.6 0.0 copy-start.3
  0.7 0.0 copy-start.5
  0.7 1.0 %copy.13 = bf16[8,16,8,112]{3,1,2,0:T(8,128)(2,1)S(1)} copy(bf16[8,16,8,112]{3,2,1,0:T(8,128)(2,1)} %param.8) | data formatting | bytes 458752 | tf_op args[1]
  1.7 0.0 copy-start
  1.7 0.0 copy-start.1
  1.7 0.1 pad.4.nb_ref
  1.8 0.0 copy-start.4
  1.8 18.6 %gather_rows.1.rows_ref = bf16[4,8,128,128]{3,2,1,0:T(8,128)(2,1)S(1)} custom-call(bf16[8,8,16,128]{3,2,1,0:T(8,128)(2,1)S(1)} %pad.4.nb_ref), custom_call_target="tpu_custom_call" | custom-call | bytes 41943040 | tf_op jit(solution)/shard_map/gather_rows/pallas_call | solution.py:193
  20.4 0.0 copy-done.2
  20.4 0.0 copy-done.3
  20.4 0.0 copy-done.5
  20.4 0.0 copy-done
  20.4 0.0 copy-done.1
  20.4 0.0 copy-done.4
  20.4 15.8 %attend_heads.1 = (bf16[128,1024]{1,0:T(8,128)(2,1)}, bf16[128,1024]{1,0:T(8,128)(2,1)}, bf16[4,8,128,128]{3,2,1,0:T(8,128)(2,1)S(1)}) custom-call(s32[2]{0:T(128)S(1)} %copy-done.4, s32[1,8]{1,0:T(1,128)S(1)} %copy-done.5, bf16[4,8,128,128]{3,2,1,0:T(8,128)(2,1)S(1)} %gather_rows.1.rows_ref, bf16[128,1024]{1,0:T(8,128)(2,1)S(1)} %copy-done.2, ...), custom_call_target="tpu_custom_call" | custom-call | tf_op jit(solution)/shard_map/attend_heads/pallas_call | solution.py:326
  36.2 14.4 %reduce_rows.1 = bf16[8,8,16,128]{3,2,1,0:T(8,128)(2,1)S(1)} custom-call(bf16[4,8,128,128]{3,2,1,0:T(8,128)(2,1)S(1)} %get-tuple-element.8.part_ref), custom_call_target="tpu_custom_call" | custom-call | tf_op jit(solution)/shard_map/reduce_rows/pallas_call | solution.py:430
  50.6 0.8 %copy.11 = bf16[8,16,8,112]{3,2,1,0:T(8,128)(2,1)} copy(bf16[8,16,8,112]{3,1,2,0:T(8,128)(2,1)S(1)} %slice_bitcast_fusion) | data formatting | bytes 458752
  (1 shorter events, 0.0 us)
Async XLA Ops:
  0.6 19.7 %copy-start.2 = (bf16[128,1024]{1,0:T(8,128)(2,1)S(1)}, bf16[128,1024]{1,0:T(8,128)(2,1)}, u32[]{:S(2)}) copy-start(bf16[128,1024]{1,0:T(8,128)(2,1)} %q_ref.1) | copy-start | bytes 786436
  0.6 19.7 %copy-start.3 = (bf16[128,1024]{1,0:T(8,128)(2,1)S(1)}, bf16[128,1024]{1,0:T(8,128)(2,1)}, u32[]{:S(2)}) copy-start(bf16[128,1024]{1,0:T(8,128)(2,1)} %g_ref.1) | copy-start | bytes 786436
  0.7 19.7 %copy-start.5 = (s32[1,8]{1,0:T(1,128)S(1)}, s32[1,8]{1,0:T(1,128)}, u32[]{:S(2)}) copy-start(s32[1,8]{1,0:T(1,128)} %slots_ref.1) | copy-start | bytes 100
  1.7 18.7 %copy-start = (bf16[448,1024]{1,0:T(8,128)(2,1)S(1)}, bf16[448,1024]{1,0:T(8,128)(2,1)}, u32[]{:S(2)}) copy-start(bf16[448,1024]{1,0:T(8,128)(2,1)} %wk_ref.1) | copy-start | bytes 2752516
  1.7 18.7 %copy-start.1 = (bf16[448,1024]{1,0:T(8,128)(2,1)S(1)}, bf16[448,1024]{1,0:T(8,128)(2,1)}, u32[]{:S(2)}) copy-start(bf16[448,1024]{1,0:T(8,128)(2,1)} %wv_ref.1) | copy-start | bytes 2752516
  1.8 18.6 %copy-start.4 = (s32[2]{0:T(128)S(1)}, s32[2]{0:T(128)}, u32[]{:S(2)}) copy-start(s32[2]{0:T(128)} %counts_ref.1) | copy-start | bytes 28
